TPU v7x, 512 devices: a whole 4x8x8 slice. The times are simulated.
512 devices in a mesh: blk: 64 (over x, z, core), rhs: 8 (over y).
Axes of the slice: x: 4, y: 8, z: 8, core: 2. Of those that a mesh axis runs over, the one named last changes fastest.
Arguments:
- rhs_vectors: float32 [64, 131072], P('rhs', 'blk'), may hold values from -6 to 6
- diag_inverse: float32 [2, 512, 256, 256], P(None, 'blk', 'rhs'), as said below
- near_left: float32 [2, 1792, 32, 256], P(None, 'blk'), may hold values from -0.375 to 0.375
- near_right: float32 [2, 1792, 32, 256], P(None, 'blk'), may hold values from -0.375 to 0.375
- near_rank: int32 [2, 1792], P(None, 'blk'), may hold values from 8 to 32
- near_pattern: int32 [2, 1792], P(None, 'blk'), may hold values 0 or 1
- far_row: float32 [2, 512, 32, 256], P(None, 'blk'), may hold values from -0.0625 to 0.0625
- far_col: float32 [2, 512, 32, 256], P(None, 'blk'), may hold values from -0.0625 to 0.0625
Outputs:
- solution: float32 [64, 131072], P('rhs', 'blk')
Inputs may be any that keep to these rules, and one draw needn't show every extreme that they name: Each tile within a group uses only its first near_rank factor rows. A tile within a group with near_pattern 0 is absent. `diag_inverse`: each block is a positive diagonal plus small entries off it.
All inputs are finite; a program needn't handle non-finite values.
Results may differ from a plain program's by a relative error of at most 0.0003.
Values sent between devices are 32-bit elements; how exact they have to be, the bound alone decides.
A program may use at most 64 MiB of HBM per device.

v0:
```python
import jax
import jax.numpy as jnp
from jax import lax
from jax.sharding import PartitionSpec as P

HIGHEST = lax.Precision.HIGHEST


def entering(value, axis, join, neutral, backward):
    count, mine = (lax.axis_size(axis), lax.axis_index(axis))
    pieces = jax.tree.map(lambda part: lax.all_gather(part, axis), value)
    if backward:
        pieces = jax.tree.map(lambda part: part[::-1], pieces)
        mine = count - 1 - mine
    running = jax.tree.map(
        lambda part, zero: jnp.full_like(part, 0) + jnp.asarray(zero, part.dtype), value, neutral
    )

    def hop(position, running):
        longer = join(running, jax.tree.map(lambda part: part[position], pieces))
        return jax.tree.map(lambda new, old: jnp.where(position < mine, new, old), longer, running)

    return lax.fori_loop(0, count - 1, hop, running)


def times_high(first, second):
    return jnp.dot(first, second, precision=HIGHEST, preferred_element_type=jnp.float32)


def times_trans(first, second):
    return lax.dot_general(
        first,
        second,
        (((1,), (1,)), ((), ())),
        precision=HIGHEST,
        preferred_element_type=jnp.float32,
    )


def pair_index(higher, lower):
    return higher * (higher - 1) // 2 + lower


def chain_combine(earlier, latter):
    return (times_high(earlier[0], latter[0]), times_high(earlier[1], latter[0]) + latter[1])


def apply_inverse(current, inverse_block):
    solved_part = times_trans(current, inverse_block)
    return solved_part


def local_part(
    side_list, inverse, left_tiles, right_tiles, keep_mask, row_gen, col_gen, block_order
):
    row_count = side_list[0].shape[0]
    rank_width = row_gen.shape[1]
    solved = {}
    finished = []
    for target in block_order:
        current = jnp.concatenate([side_list[target], -row_gen[target]], axis=0)
        for source in finished:
            pair_slot = pair_index(max(target, source), min(target, source))
            reduced = times_trans(solved[source], right_tiles[pair_slot]) * keep_mask[pair_slot]
            current = current - times_high(reduced, left_tiles[pair_slot])
        solved[target] = apply_inverse(current, inverse[target])
        finished.append(target)
    ordered = [solved[target] for target in range(len(side_list))]
    totals = times_trans(ordered[0], col_gen[0])
    for target in range(1, len(ordered)):
        totals = totals + times_trans(ordered[target], col_gen[target])
    gain_map = jnp.eye(rank_width, dtype=jnp.float32) + totals[row_count:]
    return (ordered, (gain_map, totals[:row_count]))


def finish_sweep(ordered, carried, row_count):
    return [piece[:row_count] + times_high(carried, piece[row_count:]) for piece in ordered]


def shards(
    rhs_vectors, diag_inverse, near_left, near_right, near_rank, near_pattern, far_row, far_col
):
    block_count = far_row.shape[1]
    rank_width = far_row.shape[2]
    block_width = far_row.shape[3]
    inverse = lax.all_gather(diag_inverse, "rhs", axis=2, tiled=True)
    row_count = rhs_vectors.shape[0]
    columns = lax.broadcasted_iota(jnp.int32, near_rank.shape + (rank_width,), 2)
    keep_mask = jnp.where(
        (columns < near_rank[:, :, None]) & (near_pattern[:, :, None] == 1), 1.0, 0.0
    ).astype(jnp.float32)
    identity = (
        jnp.eye(rank_width, dtype=jnp.float32),
        jnp.zeros((row_count, rank_width), jnp.float32),
    )
    side_list = [
        rhs_vectors[:, target * block_width : (target + 1) * block_width]
        for target in range(block_count)
    ]
    forward_order = list(range(block_count))
    lower_solved, lower_map = local_part(
        side_list,
        inverse[0],
        near_left[0],
        near_right[0],
        keep_mask[0],
        far_row[0],
        far_col[0],
        forward_order,
    )
    lower_prefix = entering(lower_map, "blk", chain_combine, identity, False)
    lower_out = finish_sweep(lower_solved, lower_prefix[1], row_count)
    upper_solved, upper_map = local_part(
        lower_out,
        inverse[1],
        near_left[1],
        near_right[1],
        keep_mask[1],
        far_row[1],
        far_col[1],
        forward_order[::-1],
    )
    upper_prefix = entering(upper_map, "blk", chain_combine, identity, True)
    result = jnp.concatenate(finish_sweep(upper_solved, upper_prefix[1], row_count), axis=1)
    return result


def solution(mesh):
    return jax.shard_map(
        shards,
        mesh=mesh,
        in_specs=(
            P("rhs", "blk"),
            P(None, "blk", "rhs", None),
            P(None, "blk", None, None),
            P(None, "blk", None, None),
            P(None, "blk"),
            P(None, "blk"),
            P(None, "blk", None, None),
            P(None, "blk", None, None),
        ),
        out_specs=P("rhs", "blk"),
        check_vma=False,
    )
```

profile of v0, /device:TPU:1, one launch (start us, length us, event | category | flops | bytes accessed | tf_op | source)
XLA Modules:
  0.0 392.0 jit_solution(90731278727838539)
XLA Ops:
  10.9 1.7 negate_bitcast_fusion
  12.5 59.6 %all-gather.6.cloned.1.call-done = f32[2,8,256,256]{3,2,1,0:T(8,128)} async-done(((f32[2,8,32,256]{3,2,1,0:T(8,128)}), f32[2,8,256,256]{3,2,1,0:T(8,128)}) %all-gather.6.cloned.1.call-update) | async-done | bytes 4194320 | tf_op jit(solution)/shard_map/all_gather | solution.py:86
  72.1 1.3 fusion.38
  75.6 1.3 fusion.37
  78.0 1.0 convolution_subtract_fusion.54
  80.0 1.3 fusion.36
  82.2 1.0 convolution_subtract_fusion.52
  85.1 1.3 fusion.35
  87.1 1.0 convolution_subtract_fusion.49
  88.1 1.0 convolution_subtract_fusion.48
  89.1 1.0 convolution_subtract_fusion.47
  90.1 1.0 convolution_subtract_fusion.46
  91.1 1.3 fusion.34
  92.9 1.0 convolution_subtract_fusion.45
  93.9 1.0 convolution_subtract_fusion.44
  94.9 1.0 convolution_subtract_fusion.43
  95.9 1.0 convolution_subtract_fusion.42
  96.9 1.0 convolution_subtract_fusion.41
  97.9 1.3 fusion.33
  100.6 1.0 convolution_subtract_fusion.40
  101.6 1.0 convolution_subtract_fusion.39
  102.6 1.0 convolution_subtract_fusion.38
  103.6 1.0 convolution_subtract_fusion.37
  104.6 1.0 convolution_subtract_fusion.36
  105.6 1.0 convolution_subtract_fusion.35
  106.6 1.3 fusion.32
  108.2 1.0 convolution_subtract_fusion.34
  112.2 1.0 convolution_subtract_fusion.30
  113.2 1.0 convolution_subtract_fusion.29
  115.2 1.3 fusion.31
  117.5 46.1 %all-gather.1 = f32[512,32]{1,0:T(8,128)S(1)} all-gather(f32[8,32]{1,0:T(8,128)S(1)} %copy.19), channel_id=3, replica_groups=mesh['blk'=64,'rhs'=8] {'blk'}, dimensions={0}, use_global_device_ids=true | all-gather | bytes 66560 | tf_op jit(solution)/shard_map/all_gather | solution.py:11
  163.6 49.3 %all-gather = f32[2048,32]{1,0:T(8,128)S(1)} all-gather(f32[32,32]{1,0:T(8,128)} %copy.17), channel_id=2, replica_groups=mesh['blk'=64,'rhs'=8] {'blk'}, dimensions={0}, use_global_device_ids=true | all-gather | bytes 266240 | tf_op jit(solution)/shard_map/all_gather | solution.py:11
  212.8 9.6 %while.28 = (s32[]{:T(128)}, f32[8,32]{1,0:T(8,128)S(1)}, s32[]{:T(128)}, f32[64,32,32]{2,1,0:T(8,128)S(1)}, f32[64,8,32]{2,1,0:T(8,128)S(1)}, /*index=5*/s32[]{:T(128)}, s32[]{:T(128)}) while((s32[]{:T(128)}, f32[8,32]{1,0:T(8,128)S(1)}, s32[]{:T(128)}, f32[64,32,32]{2,1,0:T(8,128)S(1)}, f32[64,8,32]{2,1,0:T(8,128)S(1)}, ...), condition=%wide.region_1.2_spmd.clone, body=%wide.region_0.1_spmd.clone.sunk | while | flops 99332 | bytes 34407 | solution.py:23
  223.6 1.3 fusion.30
  229.7 1.0 convolution_subtract_fusion.26
  230.8 1.3 fusion.29
  236.3 1.0 convolution_subtract_fusion.24
  237.3 1.0 convolution_subtract_fusion.23
  238.3 1.3 fusion.28
  242.8 1.0 convolution_subtract_fusion.21
  243.8 1.0 convolution_subtract_fusion.20
  244.8 1.0 convolution_subtract_fusion.19
  245.8 1.3 fusion.27
  247.7 1.0 convolution_subtract_fusion.17
  251.6 1.3 fusion.26
  253.3 1.0 convolution_subtract_fusion.12
  254.3 1.0 convolution_subtract_fusion.11
  255.3 1.0 convolution_subtract_fusion.10
  257.3 1.0 convolution_subtract_fusion.8
  258.4 1.3 fusion.25
  260.9 1.0 convolution_subtract_fusion.6
  262.9 1.0 convolution_subtract_fusion.4
  263.9 1.0 convolution_subtract_fusion.3
  266.9 1.3 fusion.24
  268.4 1.0 convolution_subtract_fusion.27
  269.4 1.0 convolution_subtract_fusion.25
  270.4 1.0 convolution_subtract_fusion.22
  271.4 1.0 convolution_subtract_fusion.18
  272.4 1.0 convolution_subtract_fusion.13
  273.4 1.0 convolution_subtract_fusion.7
  275.3 1.3 fusion.23
  278.3 42.2 %all-gather.3 = f32[512,32]{1,0:T(8,128)S(1)} all-gather(f32[8,32]{1,0:T(8,128)S(1)} %copy.23), channel_id=5, replica_groups=mesh['blk'=64,'rhs'=8] {'blk'}, dimensions={0}, use_global_device_ids=true | all-gather | bytes 66560 | tf_op jit(solution)/shard_map/all_gather | solution.py:11
  320.4 49.3 %all-gather.2 = f32[2048,32]{1,0:T(8,128)S(1)} all-gather(f32[32,32]{1,0:T(8,128)S(1)} %copy.21), channel_id=4, replica_groups=mesh['blk'=64,'rhs'=8] {'blk'}, dimensions={0}, use_global_device_ids=true | all-gather | bytes 266240 | tf_op jit(solution)/shard_map/all_gather | solution.py:11
  370.9 11.9 %while.29 = (s32[]{:T(128)}, f32[8,32]{1,0:T(8,128)S(1)}, s32[]{:T(128)}, f32[64,32,32]{1,0,2:T(8,128)S(1)}, f32[64,8,32]{2,1,0:T(8,128)S(1)}, /*index=5*/s32[]{:T(128)}, s32[]{:T(128)}) while((s32[]{:T(128)}, f32[8,32]{1,0:T(8,128)S(1)}, s32[]{:T(128)}, f32[64,32,32]{1,0,2:T(8,128)S(1)}, f32[64,8,32]{2,1,0:T(8,128)S(1)}, ...), condition=%wide.region_3.4_spmd.clone, body=%wide.region_2.3_spmd.clone.sunk | while | flops 99332 | bytes 42091 | solution.py:23
  (476 shorter events, 68.2 us)
Async XLA Ops:
  6.5 66.9 %copy-start = (f32[2,28,32,256]{3,2,1,0:T(8,128)S(1)}, f32[2,28,32,256]{3,2,1,0:T(8,128)}, u32[]{:S(2)}) copy-start(f32[2,28,32,256]{3,2,1,0:T(8,128)} %param.15) | copy-start | bytes 5505028
  6.5 65.6 %all-gather.6.cloned.1.call-start = ((), (), s32[]{:S(2)}) async-start(), calls=%async_computation | async-start | bytes 4718592 | tf_op jit(solution)/shard_map/all_gather | solution.py:86
  81.8 17.8 %copy-start.1 = (f32[2,8,32,256]{3,2,1,0:T(8,128)S(1)}, f32[2,8,32,256]{3,2,1,0:T(8,128)}, u32[]{:S(2)}) copy-start(f32[2,8,32,256]{3,2,1,0:T(8,128)} %param.19) | copy-start | bytes 1572868
  222.4 13.8 %copy-start.6 = (f32[32,256]{1,0:T(8,128)S(1)}, f32[32,256]{1,0:T(8,128)}, u32[]{:S(2)}) copy-start(f32[32,256]{1,0:T(8,128)} %get-tuple-element.279) | copy-start | bytes 98308
  222.4 20.4 %copy-start.5 = (f32[32,256]{1,0:T(8,128)S(1)}, f32[32,256]{1,0:T(8,128)}, u32[]{:S(2)}) copy-start(f32[32,256]{1,0:T(8,128)} %get-tuple-element.278) | copy-start | bytes 98308
  223.3 23.8 %copy-start.17 = (f32[32]{0:T(128)S(1)}, f32[32]{0:T(128)}, u32[]{:S(2)}) copy-start(f32[32]{0:T(128)} %get-tuple-element.303) | copy-start | bytes 388
  223.6 23.7 %copy-start.16 = (f32[32]{0:T(128)S(1)}, f32[32]{0:T(128)}, u32[]{:S(2)}) copy-start(f32[32]{0:T(128)} %get-tuple-element.309) | copy-start | bytes 388
  223.6 23.9 %copy-start.15 = (f32[32]{0:T(128)S(1)}, f32[32]{0:T(128)}, u32[]{:S(2)}) copy-start(f32[32]{0:T(128)} %get-tuple-element.314) | copy-start | bytes 388
  223.6 24.1 %copy-start.4 = (f32[32,256]{1,0:T(8,128)S(1)}, f32[32,256]{1,0:T(8,128)}, u32[]{:S(2)}) copy-start(f32[32,256]{1,0:T(8,128)} %get-tuple-element.277) | copy-start | bytes 98308
  230.7 22.2 %copy-start.14 = (f32[32]{0:T(128)S(1)}, f32[32]{0:T(128)}, u32[]{:S(2)}) copy-start(f32[32]{0:T(128)} %get-tuple-element.302) | copy-start | bytes 388
  230.8 22.4 %copy-start.13 = (f32[32]{0:T(128)S(1)}, f32[32]{0:T(128)}, u32[]{:S(2)}) copy-start(f32[32]{0:T(128)} %get-tuple-element.308) | copy-start | bytes 388
  232.1 21.2 %copy-start.3 = (f32[32,256]{1,0:T(8,128)S(1)}, f32[32,256]{1,0:T(8,128)}, u32[]{:S(2)}) copy-start(f32[32,256]{1,0:T(8,128)} %get-tuple-element.291) | copy-start | bytes 98308
  238.3 21.4 %copy-start.9 = (f32[32]{0:T(128)S(1)}, f32[32]{0:T(128)}, u32[]{:S(2)}) copy-start(f32[32]{0:T(128)} %get-tuple-element.301) | copy-start | bytes 388
  239.6 20.3 %copy-start.8 = (f32[32]{0:T(128)S(1)}, f32[32]{0:T(128)}, u32[]{:S(2)}) copy-start(f32[32]{0:T(128)} %get-tuple-element.307) | copy-start | bytes 388
  239.6 20.5 %copy-start.7 = (f32[32]{0:T(128)S(1)}, f32[32]{0:T(128)}, u32[]{:S(2)}) copy-start(f32[32]{0:T(128)} %get-tuple-element.313) | copy-start | bytes 388
  241.1 19.3 %copy-start.12 = (f32[32]{0:T(128)S(1)}, f32[32]{0:T(128)}, u32[]{:S(2)}) copy-start(f32[32]{0:T(128)} %get-tuple-element.322) | copy-start | bytes 388
  242.0 18.6 %copy-start.11 = (f32[32]{0:T(128)S(1)}, f32[32]{0:T(128)}, u32[]{:S(2)}) copy-start(f32[32]{0:T(128)} %get-tuple-element.325) | copy-start | bytes 388
  242.8 18.0 %copy-start.10 = (f32[32]{0:T(128)S(1)}, f32[32]{0:T(128)}, u32[]{:S(2)}) copy-start(f32[32]{0:T(128)} %get-tuple-element.327) | copy-start | bytes 388
  257.3 19.4 %copy-start.2 = (f32[2,8,32,256]{3,2,1,0:T(8,128)S(1)}, f32[2,8,32,256]{3,2,1,0:T(8,128)}, u32[]{:S(2)}) copy-start(f32[2,8,32,256]{3,2,1,0:T(8,128)} %param.19) | copy-start | bytes 1572868
  383.7 0.6 copy-start.18
Sparse Core Ops, SparseCore 0:
  9.4 62.6 all-gather.5
where the time goes:
time: 397 us; the launch traced here: 392 us
  blocking collectives  187 us (47%)
  matrix products  118 us (30%)
  waiting for transfers between devices  60.3 us (15%)
  between operations  14.8 us (4%)
  local copies, waits for them, and re-layouts  7.75 us (2%)
    all_gather x4, blocking collectives, entering(): pieces = jax.tree.map(lambda part: lax.all_gather(part, axis), value)  187 us
    dot_general x198, matrix products, times_high(): jnp.dot(first, second, precision=HIGHEST, preferred_element_type=jnp.floa...  76.1 us
    all_gather x1, waiting for transfers between devices, shards(): inverse = lax.all_gather(diag_inverse, 'rhs', axis=2, tiled=True)  59.6 us
    dot_general x88, matrix products, times_trans(): lax.dot_general(first, second, (((1,), (1,)), ((), ())), precision=HIGHES...  42.3 us
  transfers between devices with their start and end apart: 1, of which 1 were waited for; matrix products, arithmetic and copies ran while one was open for 1% of the time, Pallas kernels for 0%

commit v1 on v0

v1 whole, which is shorter than its diff:
```python
import functools

import jax
import jax.numpy as jnp
from jax import lax
from jax.experimental import pallas as pl
from jax.experimental.pallas import tpu as pltpu
from jax.sharding import PartitionSpec as P

F32 = jnp.float32
BF16 = jnp.bfloat16
MESH = pl.DeviceIdType.MESH

WIDTH = 256
RANK = 32
BLOCKS = 8
RING = 8
SHARE = WIDTH // RING
SLAB = 16
SLABS = 4
UNITS = 2 * BLOCKS
SLACK = 2
LANES = 128
PACK = LANES // RANK

ORDER = [(0, m) for m in range(BLOCKS)] + [(1, m) for m in reversed(range(BLOCKS))]


def pair_index(a, b):
    high, low = max(a, b), min(a, b)
    return high * (high - 1) // 2 + low


def hop_count(unit, side):
    return 4 if (unit + side) % 2 == 0 else 3


def parts(x):
    high = x.astype(BF16)
    return high, (x - high.astype(F32)).astype(BF16)


def times(a, b, trans):
    rows = a.shape[0]
    top = a.astype(BF16).astype(F32)
    stacked = jnp.concatenate([top, a - top], axis=0).astype(BF16)
    dims = (((1,), (1 if trans else 0,)), ((), ()))
    high, low = parts(b)
    p = lax.dot_general(stacked, high, dims, preferred_element_type=F32)
    q = lax.dot_general(stacked, low, dims, preferred_element_type=F32)
    p = p + q
    return p[:rows] + p[rows:]


def kernel(
    rhs_hbm, diag_hbm, left_hbm, right_hbm, rank_ref, pattern_ref, row_hbm, col_hbm,
    out_ref,
    rhs, inv, left, right, row, col, sol0, sol1, red, pack, xpack,
    load_sem, own_sem, ring_send, ring_recv, slab_send, slab_recv, x_send, x_recv,
):
    g = lax.axis_index("blk")
    y = lax.axis_index("rhs")
    slab, place = g // SLAB, g % SLAB

    loads = [[], []]
    loads[0].append(pltpu.make_async_copy(rhs_hbm, rhs, load_sem.at[8]))
    for s in range(2):
        for i, (src, dst) in enumerate(
            ((row_hbm, row), (col_hbm, col), (left_hbm, left), (right_hbm, right))
        ):
            loads[s].append(pltpu.make_async_copy(src.at[s], dst.at[s], load_sem.at[4 * s + i]))
    mine = pl.ds(SHARE * y, SHARE)
    own = [
        pltpu.make_async_copy(diag_hbm.at[s], inv.at[s, :, mine, :], own_sem.at[s]) for s in range(2)
    ]
    for s in range(2):
        for c in loads[s]:
            c.start()
        own[s].start()

    barrier = pltpu.get_barrier_semaphore()
    ring = ((y + 1) % RING, (y + RING - 1) % RING)
    for n in ring:
        pl.semaphore_signal(barrier, inc=1, device_id=(g, n), device_id_type=MESH)
    for d in range(1, SLAB):
        pl.semaphore_signal(
            barrier, inc=1, device_id=(slab * SLAB + (place + d) % SLAB, y), device_id_type=MESH
        )
    for d in range(1, SLABS):
        pl.semaphore_signal(
            barrier, inc=1, device_id=(((slab + d) % SLABS) * SLAB + place, y), device_id_type=MESH
        )
    pl.semaphore_wait(barrier, 2 + SLAB - 1 + SLABS - 1)

    def shard(unit, origin):
        s, m = ORDER[unit]
        return inv.at[s, m, pl.ds(SHARE * origin, SHARE), :]

    def origin_of(side, hop):
        return (y + RING - hop) % RING if side == 0 else (y + hop) % RING

    def ring_copy(unit, side, hop):
        s, m = ORDER[unit]
        there = shard(unit, origin_of(side, hop - 1) if hop > 1 else y)
        return pltpu.make_async_remote_copy(
            src_ref=diag_hbm.at[s, m] if hop == 1 else there,
            dst_ref=there,
            send_sem=ring_send.at[unit, side, hop - 1],
            recv_sem=ring_recv.at[unit, side, hop - 1],
            device_id=(g, ring[side]),
            device_id_type=MESH,
        )

    def ring_arrived(unit, side, hop):
        here = shard(unit, origin_of(side, hop))
        pltpu.make_async_remote_copy(
            src_ref=here,
            dst_ref=here,
            send_sem=ring_send.at[unit, side, hop - 1],
            recv_sem=ring_recv.at[unit, side, hop - 1],
            device_id=(g, ring[side]),
            device_id_type=MESH,
        ).wait_recv()

    lane = lax.broadcasted_iota(jnp.int32, (8, WIDTH), 1)
    slot_of, within = lane // RANK, lane % RANK
    lane128 = lax.broadcasted_iota(jnp.int32, (8, LANES), 1)
    sub128 = lax.broadcasted_iota(jnp.int32, (8, LANES), 0)
    totals = [jnp.zeros((40, LANES), F32), jnp.zeros((72, LANES), F32)]

    def solve(unit):
        s, m = ORDER[unit]
        rows = 40 if s == 0 else 72
        earlier = list(range(m)) if s == 0 else list(range(m + 1, BLOCKS))
        later = list(range(m + 1, BLOCKS)) if s == 0 else list(range(m))
        if s == 0:
            side = jnp.concatenate([rhs[:, m * WIDTH : (m + 1) * WIDTH], -row[0, m]], axis=0)
        else:
            side = jnp.concatenate([sol0[m], -row[1, m]], axis=0)
        if earlier:
            ranks = jnp.zeros((8, WIDTH), jnp.int32)
            reduced = jnp.zeros((rows, WIDTH), F32)
            for k in earlier:
                p = pair_index(m, k)
                rank = jnp.where(pattern_ref[s, p] == 1, rank_ref[s, p], 0)
                ranks = jnp.where(slot_of == (m ^ k), rank, ranks)
                hit = jnp.tile(slot_of == (m ^ k), (rows // 8, 1))
                reduced = jnp.where(hit, red[k, :rows, :], reduced)
            keep = jnp.where(within < ranks, 1.0, 0.0).astype(F32)
            reduced = reduced * jnp.tile(keep, (rows // 8, 1))
            tiles = [
                left[s, pair_index(m, m ^ j)] if (m ^ j) in earlier else jnp.zeros((RANK, WIDTH), F32)
                for j in range(BLOCKS)
            ]
            side = side - times(reduced, jnp.concatenate(tiles, axis=0), False)
        solved = times(side, inv[s, m], True)
        if s == 0:
            sol0[m] = solved
        else:
            sol1[m] = solved
        tiles = [col[s, m]] + [
            right[s, pair_index(m, m ^ j)] if (m ^ j) in later else jnp.zeros((RANK, WIDTH), F32)
            for j in range(1, BLOCKS)
        ]
        if later:
            after = times(solved, jnp.concatenate(tiles, axis=0), True)
            red[m, :rows, :] = after
            totals[s] = totals[s] + after[:, :LANES]
        else:
            after = times(solved, jnp.concatenate(tiles[:PACK], axis=0), True)
            totals[s] = totals[s] + after

    low_lanes = lane128 < RANK
    unit_pack = jnp.concatenate(
        [
            jnp.where(lane128 % RANK == sub128 + 8 * (lane128 // RANK), 1.0, 0.0).astype(F32),
            jnp.zeros((8, LANES), F32),
        ],
        axis=0,
    )

    def packed(gain_rows, v):
        a = unit_pack[:8]
        for i in range(PACK):
            piece = jnp.where(low_lanes, gain_rows[8 * i : 8 * i + 8], 0.0)
            a = a + (pltpu.roll(piece, RANK * i, 1) if i else piece)
        return jnp.concatenate([a, jnp.where(low_lanes, v, 0.0)], axis=0)

    def spread(m):
        a = m[:8]
        rolled = [a if i == 0 else pltpu.roll(a, RANK * i, 1) for i in range(PACK)]
        strips = []
        for b in range(PACK):
            for i in range(PACK):
                strips.append(jnp.where(lane128 // RANK == b, rolled[(b - i) % PACK], 0.0))
        return jnp.concatenate(strips, axis=0)

    only_v = jnp.concatenate([jnp.zeros((8, LANES), F32), jnp.ones((8, LANES), F32)], axis=0)

    def after(first, then):
        return times(first, spread(then), False) + then * only_v

    def product(maps):
        while len(maps) > 1:
            maps = [after(maps[i], maps[i + 1]) for i in range(0, len(maps), 2)]
        return maps[0]

    def slab_copy(s, d):
        return pltpu.make_async_remote_copy(
            src_ref=pack.at[s, place],
            dst_ref=pack.at[s, place],
            send_sem=slab_send.at[s, d - 1],
            recv_sem=slab_recv.at[s, d - 1],
            device_id=(slab * SLAB + (place + d) % SLAB, y),
            device_id_type=MESH,
        )

    def slab_arrived(s, d):
        here = pack.at[s, (place + SLAB - d) % SLAB]
        pltpu.make_async_remote_copy(
            src_ref=here,
            dst_ref=here,
            send_sem=slab_send.at[s, d - 1],
            recv_sem=slab_recv.at[s, d - 1],
            device_id=(slab * SLAB + (place + d) % SLAB, y),
            device_id_type=MESH,
        ).wait_recv()

    def x_copy(s, d):
        return pltpu.make_async_remote_copy(
            src_ref=xpack.at[s, slab],
            dst_ref=xpack.at[s, slab],
            send_sem=x_send.at[s, d - 1],
            recv_sem=x_recv.at[s, d - 1],
            device_id=(((slab + d) % SLABS) * SLAB + place, y),
            device_id_type=MESH,
        )

    def x_arrived(s, d):
        here = xpack.at[s, (slab + SLABS - d) % SLABS]
        pltpu.make_async_remote_copy(
            src_ref=here,
            dst_ref=here,
            send_sem=x_send.at[s, d - 1],
            recv_sem=x_recv.at[s, d - 1],
            device_id=(((slab + d) % SLABS) * SLAB + place, y),
            device_id_type=MESH,
        ).wait_recv()

    def exchange_start(s, packet):
        pack[s, place] = packet
        for d in range(1, SLAB):
            slab_copy(s, d).start()

    def exchange_middle(s):
        for d in range(1, SLAB):
            slab_arrived(s, d)
        order = list(range(SLAB)) if s == 0 else list(reversed(range(SLAB)))
        maps = [pack[s, i] for i in order]
        whole = product(maps)
        xpack[s, slab] = whole
        for d in range(1, SLABS):
            x_copy(s, d).start()
        ahead = [
            jnp.where((place > i) if s == 0 else (place < i), one, unit_pack)
            for i, one in zip(order, maps)
        ]
        return product(ahead)

    def exchange_end(s, ahead):
        for d in range(1, SLABS):
            x_arrived(s, d)
        order = list(range(SLABS)) if s == 0 else list(reversed(range(SLABS)))
        maps = [
            jnp.where((slab > i) if s == 0 else (slab < i), xpack[s, i], unit_pack) for i in order
        ]
        entering = product([product(maps), ahead])
        return entering[8:]

    lower_ready = {}
    span = 4 * SLACK
    carried = None
    for tick in range(UNITS + span):
        for hop in (4, 3, 2, 1):
            unit = tick - SLACK * (hop - 1)
            if not 0 <= unit < UNITS:
                continue
            for side in range(2):
                if hop > hop_count(unit, side):
                    continue
                if hop > 1:
                    ring_arrived(unit, side, hop - 1)
                ring_copy(unit, side, hop).start()
        unit = tick - span
        if unit < 0:
            continue
        if unit == 0:
            for c in loads[0]:
                c.wait()
            own[0].wait()
        if unit == BLOCKS:
            for c in loads[1]:
                c.wait()
            own[1].wait()
        for side in range(2):
            ring_arrived(unit, side, hop_count(unit, side))
        solve(unit)
        if unit == BLOCKS - 1:
            exchange_start(0, packed(totals[0][8:40], totals[0][:8]))
        if unit == BLOCKS + 2:
            lower_ready["ahead"] = exchange_middle(0)
        if unit == BLOCKS + 5:
            carried = exchange_end(0, lower_ready["ahead"])

    upper_v = totals[1][:8] + times(carried[:, :RANK], totals[1][8:40], False)
    exchange_start(1, packed(totals[1][40:72], upper_v))
    entering = exchange_end(1, exchange_middle(1))

    both = carried + pltpu.roll(entering, RANK, 1)
    for m in range(BLOCKS):
        out_ref[:, m * WIDTH : (m + 1) * WIDTH] = sol1[m, 0:8, :] + times(
            both[:, : 2 * RANK], sol1[m, 8:72, :], False
        )

    for unit in range(UNITS):
        for side in range(2):
            for hop in range(1, hop_count(unit, side) + 1):
                ring_copy(unit, side, hop).wait_send()
    for s in range(2):
        for d in range(1, SLAB):
            slab_copy(s, d).wait_send()
        for d in range(1, SLABS):
            x_copy(s, d).wait_send()


def shards(rhs, diag, left, right, rank, pattern, row, col):
    hbm = pl.BlockSpec(memory_space=pl.ANY)
    smem = pl.BlockSpec(memory_space=pltpu.SMEM)
    return pl.pallas_call(
        kernel,
        out_shape=jax.ShapeDtypeStruct(rhs.shape, F32),
        in_specs=[hbm, hbm, hbm, hbm, smem, smem, hbm, hbm],
        out_specs=pl.BlockSpec(memory_space=pltpu.VMEM),
        scratch_shapes=[
            pltpu.VMEM(rhs.shape, F32),
            pltpu.VMEM((2, BLOCKS, WIDTH, WIDTH), F32),
            pltpu.VMEM(left.shape, F32),
            pltpu.VMEM(right.shape, F32),
            pltpu.VMEM(row.shape, F32),
            pltpu.VMEM(col.shape, F32),
            pltpu.VMEM((BLOCKS, 40, WIDTH), F32),
            pltpu.VMEM((BLOCKS, 72, WIDTH), F32),
            pltpu.VMEM((BLOCKS, 72, WIDTH), F32),
            pltpu.VMEM((2, SLAB, 16, LANES), F32),
            pltpu.VMEM((2, SLABS, 16, LANES), F32),
            pltpu.SemaphoreType.DMA((9,)),
            pltpu.SemaphoreType.DMA((2,)),
            pltpu.SemaphoreType.DMA((UNITS, 2, 4)),
            pltpu.SemaphoreType.DMA((UNITS, 2, 4)),
            pltpu.SemaphoreType.DMA((2, SLAB - 1)),
            pltpu.SemaphoreType.DMA((2, SLAB - 1)),
            pltpu.SemaphoreType.DMA((2, SLABS - 1)),
            pltpu.SemaphoreType.DMA((2, SLABS - 1)),
        ],
        compiler_params=pltpu.CompilerParams(
            collective_id=0, has_side_effects=True, vmem_limit_bytes=40 * 1024 * 1024
        ),
        cost_estimate=pl.CostEstimate(
            flops=400_000_000, bytes_accessed=6_000_000, transcendentals=0
        ),
    )(rhs, diag, left, right, rank, pattern, row, col)


def solution(mesh):
    return jax.shard_map(
        shards,
        mesh=mesh,
        in_specs=(
            P("rhs", "blk"),
            P(None, "blk", "rhs", None),
            P(None, "blk", None, None),
            P(None, "blk", None, None),
            P(None, "blk"),
            P(None, "blk"),
            P(None, "blk", None, None),
            P(None, "blk", None, None),
        ),
        out_specs=P("rhs", "blk"),
        check_vma=False,
    )
```

time: 397 us -> 88.5 us (0.22); the launches traced: 392 us -> 88.1 us
  blocking collectives: 187 us -> 0 us
  matrix products: 118 us -> 0 us
  Pallas kernels: 0 us -> 79.1 us
  waiting for transfers between devices: 60.3 us -> 0 us
  between operations: 14.8 us -> 0.02 us
    all_gather x4 -> x0, blocking collectives: 187 us -> none  [entering(): pieces = jax.tree.map(lambda part: lax.all_gather(part, axis), value)]
    dot_general x286 -> x0, matrix products: 118 us -> none  [the longest x198 76.1 us: times_high(): jnp.dot(first, second, precision=HIGHEST, preferred_element_type=jnp.floa...]
    pallas_call x0 -> x1, Pallas kernels: none -> 79.1 us  [shards(): pl.pallas_call(kernel, out_shape=jax.ShapeDtypeStruct(rhs.shape, F32), in...]
    all_gather x1 -> x0, waiting for transfers between devices: 59.6 us -> none  [shards(): inverse = lax.all_gather(diag_inverse, 'rhs', axis=2, tiled=True)]
    unnamed x38 -> x17, local copies, waits for them, and re-layouts: 0.74 us -> 8.95 us
  transfers between devices with their start and end apart: 1 -> 0, of which waited for: 1 -> 0; matrix products, arithmetic and copies ran while one was open for 1% -> 0% of each run, Pallas kernels for 0% -> 0%
where the time goes in v1:
time: 88.5 us; the launch traced here: 88.1 us
  Pallas kernels  79.1 us (89%)
  local copies, waits for them, and re-layouts  8.95 us (10%)
    pallas_call x1, Pallas kernels, shards(): pl.pallas_call(kernel, out_shape=jax.ShapeDtypeStruct(rhs.shape, F32), in...  79.1 us
    unnamed x17, local copies, waits for them, and re-layouts  8.95 us

profile of v1, /device:TPU:1, one launch (start us, length us, event | category | flops | bytes accessed | tf_op | source)
XLA Modules:
  0.0 88.1 jit_solution(10877221304302181916)
XLA Ops:
  0.0 0.0 copy-start
  0.0 1.5 %copy-done = f32[2,28,32,256]{3,2,1,0:T(8,128)S(1)} copy-done((f32[2,28,32,256]{3,2,1,0:T(8,128)S(1)}, f32[2,28,32,256]{3,2,1,0:T(8,128)}, u32[]{:S(2)}) %copy-start) | copy-done | bytes 1835032
  1.5 0.0 copy-start.1
  1.5 1.5 %copy-done.1 = f32[2,28,32,256]{3,2,1,0:T(8,128)S(1)} copy-done((f32[2,28,32,256]{3,2,1,0:T(8,128)S(1)}, f32[2,28,32,256]{3,2,1,0:T(8,128)}, u32[]{:S(2)}) %copy-start.1) | copy-done | bytes 1835032
  3.0 0.0 copy-start.2
  3.0 1.0 %copy-done.2 = f32[2,8,32,256]{3,2,1,0:T(8,128)S(1)} copy-done((f32[2,8,32,256]{3,2,1,0:T(8,128)S(1)}, f32[2,8,32,256]{3,2,1,0:T(8,128)}, u32[]{:S(2)}) %copy-start.2) | copy-done | bytes 524312
  4.0 0.0 copy-start.3
  4.0 1.0 %copy-done.3 = f32[2,8,32,256]{3,2,1,0:T(8,128)S(1)} copy-done((f32[2,8,32,256]{3,2,1,0:T(8,128)S(1)}, f32[2,8,32,256]{3,2,1,0:T(8,128)}, u32[]{:S(2)}) %copy-start.3) | copy-done | bytes 524312
  5.1 0.0 copy-start.4
  5.1 1.0 %copy-done.4 = f32[2,8,32,256]{3,2,1,0:T(8,128)S(1)} copy-done((f32[2,8,32,256]{3,2,1,0:T(8,128)S(1)}, f32[2,8,32,256]{3,2,1,0:T(8,128)}, u32[]{:S(2)}) %copy-start.4) | copy-done | bytes 524312
  6.1 0.0 copy-start.5
  6.1 0.8 copy-done.5
  7.0 0.0 copy-start.6
  7.0 0.7 copy-done.6
  7.6 0.0 copy-start.7
  7.6 0.7 copy-done.7
  8.3 79.1 %shard_map.82 = f32[8,2048]{1,0:T(8,128)S(1)} custom-call(f32[8,2048]{1,0:T(8,128)S(1)} %copy-done.5, f32[2,8,32,256]{3,2,1,0:T(8,128)S(1)} %copy-done.2, f32[2,28,32,256]{3,2,1,0:T(8,128)S(1)} %copy-done, f32[2,28,32,256]{3,2,1,0:T(8,128)S(1)} %copy-done.1, s32[2,28]{1,0:T(2,128)S(1)} %copy-done.6, s32[2,28]{1,0:T(2,128)S(1)} %copy-done.7, ...), custom_call_target="tpu_custom_call" | custom-call | flops 400000000 | bytes 6000000 | tf_op jit(solution)/shard_map/pallas_call | solution.py:339
  87.5 0.6 copy.10
Async XLA Ops:
  0.0 1.5 %copy-start = (f32[2,28,32,256]{3,2,1,0:T(8,128)S(1)}, f32[2,28,32,256]{3,2,1,0:T(8,128)}, u32[]{:S(2)}) copy-start(f32[2,28,32,256]{3,2,1,0:T(8,128)} %left_hbm.1) | copy-start | bytes 5505028
  1.5 1.5 %copy-start.1 = (f32[2,28,32,256]{3,2,1,0:T(8,128)S(1)}, f32[2,28,32,256]{3,2,1,0:T(8,128)}, u32[]{:S(2)}) copy-start(f32[2,28,32,256]{3,2,1,0:T(8,128)} %right_hbm.1) | copy-start | bytes 5505028
  3.0 1.0 %copy-start.2 = (f32[2,8,32,256]{3,2,1,0:T(8,128)S(1)}, f32[2,8,32,256]{3,2,1,0:T(8,128)}, u32[]{:S(2)}) copy-start(f32[2,8,32,256]{3,2,1,0:T(8,128)} %diag_hbm.1) | copy-start | bytes 1572868
  4.0 1.0 %copy-start.3 = (f32[2,8,32,256]{3,2,1,0:T(8,128)S(1)}, f32[2,8,32,256]{3,2,1,0:T(8,128)}, u32[]{:S(2)}) copy-start(f32[2,8,32,256]{3,2,1,0:T(8,128)} %row_hbm.1) | copy-start | bytes 1572868
  5.1 1.0 %copy-start.4 = (f32[2,8,32,256]{3,2,1,0:T(8,128)S(1)}, f32[2,8,32,256]{3,2,1,0:T(8,128)}, u32[]{:S(2)}) copy-start(f32[2,8,32,256]{3,2,1,0:T(8,128)} %col_hbm.1) | copy-start | bytes 1572868
  6.1 0.8 copy-start.5
  7.0 0.7 copy-start.6
  7.6 0.7 copy-start.7

commit v2 on v1

v2 whole, which is shorter than its diff:
```python
import functools

import jax
import jax.numpy as jnp
from jax import lax
from jax.experimental import pallas as pl
from jax.experimental.pallas import tpu as pltpu
from jax.sharding import PartitionSpec as P

F32 = jnp.float32
BF16 = jnp.bfloat16
MESH = pl.DeviceIdType.MESH

WIDTH = 256
RANK = 32
BLOCKS = 8
RING = 8
ROWS = 8
ALL = ROWS * RING
LOWER = ALL + RANK
UPPER = LOWER + RANK
SHARE = WIDTH // RING
SLAB = 16
SLABS = 4
UNITS = 2 * BLOCKS
LANES = 128
PACK = LANES // RANK
VROWS = ALL // PACK
MAP = 8 + VROWS
HALVES = 2

ORDER = [(0, m) for m in range(BLOCKS)] + [(1, m) for m in reversed(range(BLOCKS))]


def pair_index(a, b):
    high, low = max(a, b), min(a, b)
    return high * (high - 1) // 2 + low


def parts(x):
    high = x.astype(BF16)
    return high, (x - high.astype(F32)).astype(BF16)


def times(a, b, trans):
    rows = a.shape[0]
    top = a.astype(BF16).astype(F32)
    stacked = jnp.concatenate([top, a - top], axis=0).astype(BF16)
    dims = (((1,), (1 if trans else 0,)), ((), ()))
    high, low = parts(b)
    p = lax.dot_general(stacked, high, dims, preferred_element_type=F32)
    q = lax.dot_general(stacked, low, dims, preferred_element_type=F32)
    p = p + q
    return p[:rows] + p[rows:]


def kernel(
    rhs_hbm, diag_hbm, left_hbm, right_hbm, rank_ref, pattern_ref, row_hbm, col_hbm,
    out_ref,
    rhs, inv, left, right, row, col, sol0, sol1, red, pack, xpack, result,
    load_sem, own_sem, unit_send, unit_recv, rhs_send, rhs_recv,
    slab_send, slab_recv, x_send, x_recv, out_send, out_recv, out_own,
):
    g = lax.axis_index("blk")
    y = lax.axis_index("rhs")
    slab, place = g // SLAB, g % SLAB
    home = (RING // 2) * (g % 2)
    barrier = pltpu.get_barrier_semaphore()

    def unit_copy(unit, origin):
        s, m = ORDER[unit]
        return pltpu.make_async_remote_copy(
            src_ref=diag_hbm.at[s, m],
            dst_ref=inv.at[s, m, pl.ds(SHARE * origin, SHARE), :],
            send_sem=unit_send.at[unit],
            recv_sem=unit_recv.at[unit, (origin - home + RING) % RING - 1],
            device_id=(g, home),
            device_id_type=MESH,
        )

    def rhs_copy(origin):
        return pltpu.make_async_remote_copy(
            src_ref=rhs_hbm,
            dst_ref=rhs.at[pl.ds(ROWS * origin, ROWS), :],
            send_sem=rhs_send,
            recv_sem=rhs_recv.at[(origin - home + RING) % RING - 1],
            device_id=(g, home),
            device_id_type=MESH,
        )

    width = out_ref.shape[1] // HALVES

    def out_copy(half, d):
        n = (home + d) % RING
        return pltpu.make_async_remote_copy(
            src_ref=result.at[pl.ds(ROWS * n, ROWS), pl.ds(half * width, width)],
            dst_ref=out_ref.at[:, pl.ds(half * width, width)],
            send_sem=out_send.at[half, d - 1],
            recv_sem=out_recv.at[half],
            device_id=(g, n),
            device_id_type=MESH,
        )

    @pl.when(y != home)
    def _():
        pl.semaphore_signal(barrier, inc=1, device_id=(g, home), device_id_type=MESH)
        pl.semaphore_wait(barrier, 1)
        rhs_copy(y).start()
        for unit in range(UNITS):
            unit_copy(unit, y).start()
        rhs_copy(y).wait_send()
        for unit in range(UNITS):
            unit_copy(unit, y).wait_send()
        for half in range(HALVES):
            out_copy(half, 1).wait_recv()

    @pl.when(y == home)
    def _():
        solve_group(
            g, y, slab, place, home, barrier, unit_copy, rhs_copy, out_copy,
            rhs_hbm, diag_hbm, left_hbm, right_hbm, rank_ref, pattern_ref, row_hbm, col_hbm,
            out_ref,
            rhs, inv, left, right, row, col, sol0, sol1, red, pack, xpack, result,
            load_sem, own_sem, slab_send, slab_recv, x_send, x_recv, out_own,
        )


def solve_group(
    g, y, slab, place, home, barrier, unit_copy, rhs_copy, out_copy,
    rhs_hbm, diag_hbm, left_hbm, right_hbm, rank_ref, pattern_ref, row_hbm, col_hbm,
    out_ref,
    rhs, inv, left, right, row, col, sol0, sol1, red, pack, xpack, result,
    load_sem, own_sem, slab_send, slab_recv, x_send, x_recv, out_own,
):
    for d in range(1, RING):
        pl.semaphore_signal(
            barrier, inc=1, device_id=(g, (home + d) % RING), device_id_type=MESH
        )

    def slab_peer(d):
        there = (place + d) % SLAB
        return (slab * SLAB + there, (RING // 2) * (there % 2))

    def x_peer(d):
        return (((slab + d) % SLABS) * SLAB + place, home)

    for d in range(1, SLAB):
        pl.semaphore_signal(barrier, inc=1, device_id=slab_peer(d), device_id_type=MESH)
    for d in range(1, SLABS):
        pl.semaphore_signal(barrier, inc=1, device_id=x_peer(d), device_id_type=MESH)

    loads = [[], []]
    loads[0].append(
        pltpu.make_async_copy(rhs_hbm, rhs.at[pl.ds(ROWS * y, ROWS), :], load_sem.at[8])
    )
    for s in range(2):
        for i, (src, dst) in enumerate(
            ((row_hbm, row), (col_hbm, col), (left_hbm, left), (right_hbm, right))
        ):
            loads[s].append(pltpu.make_async_copy(src.at[s], dst.at[s], load_sem.at[4 * s + i]))
        loads[s].append(
            pltpu.make_async_copy(
                diag_hbm.at[s], inv.at[s, :, pl.ds(SHARE * y, SHARE), :], own_sem.at[s]
            )
        )
    for s in range(2):
        for c in loads[s]:
            c.start()

    lane = lax.broadcasted_iota(jnp.int32, (8, WIDTH), 1)
    slot_of, within = lane // RANK, lane % RANK
    lane128 = lax.broadcasted_iota(jnp.int32, (8, LANES), 1)
    sub128 = lax.broadcasted_iota(jnp.int32, (8, LANES), 0)
    totals = [jnp.zeros((LOWER, LANES), F32), jnp.zeros((UPPER, LANES), F32)]

    def solve(unit):
        s, m = ORDER[unit]
        rows = LOWER if s == 0 else UPPER
        earlier = list(range(m)) if s == 0 else list(range(m + 1, BLOCKS))
        later = list(range(m + 1, BLOCKS)) if s == 0 else list(range(m))
        if s == 0:
            side = jnp.concatenate([rhs[:, m * WIDTH : (m + 1) * WIDTH], -row[0, m]], axis=0)
        else:
            side = jnp.concatenate([sol0[m], -row[1, m]], axis=0)
        if earlier:
            ranks = jnp.zeros((8, WIDTH), jnp.int32)
            reduced = jnp.zeros((rows, WIDTH), F32)
            for k in earlier:
                p = pair_index(m, k)
                rank = jnp.where(pattern_ref[s, p] == 1, rank_ref[s, p], 0)
                ranks = jnp.where(slot_of == (m ^ k), rank, ranks)
                hit = jnp.tile(slot_of == (m ^ k), (rows // 8, 1))
                reduced = jnp.where(hit, red[k, :rows, :], reduced)
            keep = jnp.where(within < ranks, 1.0, 0.0).astype(F32)
            reduced = reduced * jnp.tile(keep, (rows // 8, 1))
            tiles = [
                left[s, pair_index(m, m ^ j)] if (m ^ j) in earlier else jnp.zeros((RANK, WIDTH), F32)
                for j in range(BLOCKS)
            ]
            side = side - times(reduced, jnp.concatenate(tiles, axis=0), False)
        for d in range(1, RING):
            unit_copy(unit, (home + d) % RING).wait_recv()
        solved = times(side, inv[s, m], True)
        if s == 0:
            sol0[m] = solved
        else:
            sol1[m] = solved
        tiles = [col[s, m]] + [
            right[s, pair_index(m, m ^ j)] if (m ^ j) in later else jnp.zeros((RANK, WIDTH), F32)
            for j in range(1, BLOCKS)
        ]
        if later:
            after = times(solved, jnp.concatenate(tiles, axis=0), True)
            red[m, :rows, :] = after
            totals[s] = totals[s] + after[:, :LANES]
        else:
            after = times(solved, jnp.concatenate(tiles[:PACK], axis=0), True)
            totals[s] = totals[s] + after

    low_lanes = lane128 < RANK
    low_tall = jnp.tile(low_lanes, (ALL // 8, 1))
    unit_pack = jnp.concatenate(
        [
            jnp.where(lane128 % RANK == sub128 + 8 * (lane128 // RANK), 1.0, 0.0).astype(F32),
            jnp.zeros((VROWS, LANES), F32),
        ],
        axis=0,
    )
    only_v = jnp.concatenate([jnp.zeros((8, LANES), F32), jnp.ones((VROWS, LANES), F32)], axis=0)

    def turned(x, groups):
        groups = groups % PACK
        return pltpu.roll(x, RANK * groups, 1) if groups else x

    def beside(x, group_rows):
        x = jnp.where(low_tall[: x.shape[0]], x, 0.0)
        total = x[:group_rows]
        for i in range(1, PACK):
            total = total + turned(x[group_rows * i : group_rows * (i + 1)], i)
        return total

    def packed(gain_rows, v):
        return jnp.concatenate([unit_pack[:8] + beside(gain_rows, 8), beside(v, VROWS)], axis=0)

    def below(v):
        stacked = jnp.concatenate([turned(v, PACK - i) for i in range(PACK)], axis=0)
        return jnp.where(low_tall, stacked, 0.0)

    def spread(m):
        a = m[:8]
        rolled = [turned(a, i) for i in range(PACK)]
        strips = []
        for b in range(PACK):
            for i in range(PACK):
                strips.append(jnp.where(lane128 // RANK == b, rolled[(b - i) % PACK], 0.0))
        return jnp.concatenate(strips, axis=0)

    def after(first, then):
        return times(first, spread(then), False) + then * only_v

    def slab_copy(s, d):
        return pltpu.make_async_remote_copy(
            src_ref=pack.at[s, place],
            dst_ref=pack.at[s, place],
            send_sem=slab_send.at[s, d - 1],
            recv_sem=slab_recv.at[s, d - 1],
            device_id=slab_peer(d),
            device_id_type=MESH,
        )

    def slab_arrived(s, d):
        here = pack.at[s, (place + SLAB - d) % SLAB]
        pltpu.make_async_remote_copy(
            src_ref=here,
            dst_ref=here,
            send_sem=slab_send.at[s, d - 1],
            recv_sem=slab_recv.at[s, d - 1],
            device_id=slab_peer(d),
            device_id_type=MESH,
        ).wait_recv()

    def x_copy(s, d):
        return pltpu.make_async_remote_copy(
            src_ref=xpack.at[s, slab],
            dst_ref=xpack.at[s, slab],
            send_sem=x_send.at[s, d - 1],
            recv_sem=x_recv.at[s, d - 1],
            device_id=x_peer(d),
            device_id_type=MESH,
        )

    def x_arrived(s, d):
        here = xpack.at[s, (slab + SLABS - d) % SLABS]
        pltpu.make_async_remote_copy(
            src_ref=here,
            dst_ref=here,
            send_sem=x_send.at[s, d - 1],
            recv_sem=x_recv.at[s, d - 1],
            device_id=x_peer(d),
            device_id_type=MESH,
        ).wait_recv()

    def exchange_start(s, packet):
        pack[s, place] = packet
        for d in range(1, SLAB):
            slab_copy(s, d).start()

    def exchange_middle(s):
        for d in range(1, SLAB):
            slab_arrived(s, d)
        mine = place if s == 0 else SLAB - 1 - place
        nodes = [pack[s, i if s == 0 else SLAB - 1 - i] for i in range(SLAB)]
        ahead = None
        while len(nodes) > 1:
            left_one = unit_pack
            size = SLAB // len(nodes)
            for i in range(0, len(nodes), 2):
                at = mine // size == i + 1
                left_one = jnp.where(at, nodes[i], left_one)
            nodes = [after(nodes[i], nodes[i + 1]) for i in range(0, len(nodes), 2)]
            ahead = left_one if ahead is None else after(left_one, ahead)
        xpack[s, slab] = nodes[0]
        for d in range(1, SLABS):
            x_copy(s, d).start()
        return ahead

    def exchange_end(s, ahead):
        wide = spread(ahead)
        for d in range(1, SLABS):
            x_arrived(s, d)
        order = list(range(SLABS)) if s == 0 else list(reversed(range(SLABS)))
        maps = [
            jnp.where((slab > i) if s == 0 else (slab < i), xpack[s, i], unit_pack) for i in order
        ]
        entering = maps[0][8:]
        for one in maps[1 : SLABS - 1]:
            entering = times(entering, spread(one), False) + one[8:]
        return times(entering, wide, False) + ahead[8:]

    ahead, carried = None, None
    for unit in range(UNITS):
        if unit == 0:
            for c in loads[0]:
                c.wait()
            for d in range(1, RING):
                rhs_copy((home + d) % RING).wait_recv()
        if unit == BLOCKS:
            for c in loads[1]:
                c.wait()
        solve(unit)
        if unit == BLOCKS - 1:
            pl.semaphore_wait(barrier, RING - 1 + SLAB - 1 + SLABS - 1)
            exchange_start(0, packed(totals[0][ALL:], totals[0][:ALL]))
        if unit == BLOCKS + 2:
            ahead = exchange_middle(0)
        if unit == BLOCKS + 5:
            carried = below(exchange_end(0, ahead))

    upper_v = totals[1][:ALL] + times(carried[:, :RANK], totals[1][ALL:LOWER], False)
    exchange_start(1, packed(totals[1][LOWER:], upper_v))
    entering = below(exchange_end(1, exchange_middle(1)))

    both = (carried + turned(entering, 1))[:, : 2 * RANK]
    own = []
    for half in range(HALVES):
        for m in range(half * BLOCKS // HALVES, (half + 1) * BLOCKS // HALVES):
            result[:, m * WIDTH : (m + 1) * WIDTH] = sol1[m, :ALL, :] + times(
                both, sol1[m, ALL:, :], False
            )
        for d in range(1, RING):
            out_copy(half, d).start()
        part = pl.ds(half * (BLOCKS // HALVES) * WIDTH, (BLOCKS // HALVES) * WIDTH)
        own.append(
            pltpu.make_async_copy(
                result.at[pl.ds(ROWS * y, ROWS), part], out_ref.at[:, part], out_own.at[half]
            )
        )
        own[half].start()

    for s in range(2):
        for d in range(1, SLAB):
            slab_copy(s, d).wait_send()
        for d in range(1, SLABS):
            x_copy(s, d).wait_send()
    for half in range(HALVES):
        own[half].wait()
        for d in range(1, RING):
            out_copy(half, d).wait_send()


def shards(rhs, diag, left, right, rank, pattern, row, col):
    hbm = pl.BlockSpec(memory_space=pl.ANY)
    smem = pl.BlockSpec(memory_space=pltpu.SMEM)
    return pl.pallas_call(
        kernel,
        out_shape=jax.ShapeDtypeStruct(rhs.shape, F32),
        in_specs=[hbm, hbm, hbm, hbm, smem, smem, hbm, hbm],
        out_specs=hbm,
        scratch_shapes=[
            pltpu.VMEM((ALL, rhs.shape[1]), F32),
            pltpu.VMEM((2, BLOCKS, WIDTH, WIDTH), F32),
            pltpu.VMEM(left.shape, F32),
            pltpu.VMEM(right.shape, F32),
            pltpu.VMEM(row.shape, F32),
            pltpu.VMEM(col.shape, F32),
            pltpu.VMEM((BLOCKS, LOWER, WIDTH), F32),
            pltpu.VMEM((BLOCKS, UPPER, WIDTH), F32),
            pltpu.VMEM((BLOCKS, UPPER, WIDTH), F32),
            pltpu.VMEM((2, SLAB, MAP, LANES), F32),
            pltpu.VMEM((2, SLABS, MAP, LANES), F32),
            pltpu.VMEM((ALL, rhs.shape[1]), F32),
            pltpu.SemaphoreType.DMA((9,)),
            pltpu.SemaphoreType.DMA((2,)),
            pltpu.SemaphoreType.DMA((UNITS,)),
            pltpu.SemaphoreType.DMA((UNITS, RING - 1)),
            pltpu.SemaphoreType.DMA,
            pltpu.SemaphoreType.DMA((RING - 1,)),
            pltpu.SemaphoreType.DMA((2, SLAB - 1)),
            pltpu.SemaphoreType.DMA((2, SLAB - 1)),
            pltpu.SemaphoreType.DMA((2, SLABS - 1)),
            pltpu.SemaphoreType.DMA((2, SLABS - 1)),
            pltpu.SemaphoreType.DMA((HALVES, RING - 1)),
            pltpu.SemaphoreType.DMA((HALVES,)),
            pltpu.SemaphoreType.DMA((HALVES,)),
        ],
        compiler_params=pltpu.CompilerParams(
            collective_id=0, has_side_effects=True, vmem_limit_bytes=60 * 1024 * 1024
        ),
        cost_estimate=pl.CostEstimate(
            flops=400_000_000, bytes_accessed=6_000_000, transcendentals=0
        ),
    )(rhs, diag, left, right, rank, pattern, row, col)


def solution(mesh):
    return jax.shard_map(
        shards,
        mesh=mesh,
        in_specs=(
            P("rhs", "blk"),
            P(None, "blk", "rhs", None),
            P(None, "blk", None, None),
            P(None, "blk", None, None),
            P(None, "blk"),
            P(None, "blk"),
            P(None, "blk", None, None),
            P(None, "blk", None, None),
        ),
        out_specs=P("rhs", "blk"),
        check_vma=False,
    )
```

time: 88.5 us -> 77.7 us (0.88)
  local copies, waits for them, and re-layouts: 8.95 us -> 1.47 us
  Pallas kernels: 79.1 us -> 76.1 us
    unnamed x17 -> x1, local copies, waits for them, and re-layouts: 8.95 us -> 1.47 us
    pallas_call x1, Pallas kernels: 79.1 us -> 76.1 us  [shards(): pl.pallas_call(kernel, out_shape=jax.ShapeDtypeStruct(rhs.shape, F32), in...]
where the time goes in v2:
time: 77.7 us; the launch traced here: 77.6 us
  Pallas kernels  76.1 us (98%)
  local copies, waits for them, and re-layouts  1.47 us (2%)
    pallas_call x1, Pallas kernels, shards(): pl.pallas_call(kernel, out_shape=jax.ShapeDtypeStruct(rhs.shape, F32), in...  76.1 us

profile of v2, /device:TPU:1, one launch (start us, length us, event | category | flops | bytes accessed | tf_op | source)
XLA Modules:
  0.0 77.6 jit_solution(15522991615448826568)
XLA Ops:
  0.0 76.1 %shard_map.82 = f32[8,2048]{1,0:T(8,128)} custom-call(f32[8,2048]{1,0:T(8,128)} %rhs_hbm.1, f32[2,8,32,256]{3,2,1,0:T(8,128)} %diag_hbm.1, f32[2,28,32,256]{3,2,1,0:T(8,128)} %left_hbm.1, f32[2,28,32,256]{3,2,1,0:T(8,128)} %right_hbm.1, s32[2,28]{1,0:T(2,128)} %rank_ref.1, s32[2,28]{1,0:T(2,128)} %pattern_ref.1, f32[2,8,32,256]{3,2,1,0:T(8,128)} %row_hbm.1, ...), custom_call_target="tpu_custom_call" | custom-call | flops 400000000 | bytes 6000000 | tf_op jit(solution)/shard_map/pallas_call | solution.py:394
  76.1 1.5 %copy.10 = f32[8,2048]{1,0:T(8,128)} copy(f32[8,2048]{1,0:T(8,128)} %shard_map.82) | data formatting | bytes 131072

commit v3 on v2

v3 whole, which is shorter than its diff:
```python
import functools

import jax
import jax.numpy as jnp
from jax import lax
from jax.experimental import pallas as pl
from jax.experimental.pallas import tpu as pltpu
from jax.sharding import PartitionSpec as P

F32 = jnp.float32
BF16 = jnp.bfloat16
MESH = pl.DeviceIdType.MESH

WIDTH = 256
RANK = 32
BLOCKS = 8
RING = 8
ROWS = 8
ALL = ROWS * RING
LOWER = ALL + RANK
UPPER = LOWER + RANK
SHARE = WIDTH // RING
OCTET = 8
UNITS = 2 * BLOCKS
LANES = 128
PACK = LANES // RANK
VROWS = ALL // PACK
MAP = 8 + VROWS
PARTS = 4
WINDOW = 6
STRIDE = 2

ORDER = [(0, m) for m in range(BLOCKS)] + [(1, m) for m in reversed(range(BLOCKS))]


def pair_index(a, b):
    high, low = max(a, b), min(a, b)
    return high * (high - 1) // 2 + low


def parts(x):
    high = x.astype(BF16)
    return high, (x - high.astype(F32)).astype(BF16)


def times(a, b, trans):
    rows = a.shape[0]
    top = a.astype(BF16).astype(F32)
    stacked = jnp.concatenate([top, a - top], axis=0).astype(BF16)
    dims = (((1,), (1 if trans else 0,)), ((), ()))
    high, low = parts(b)
    p = lax.dot_general(stacked, high, dims, preferred_element_type=F32)
    q = lax.dot_general(a.astype(BF16), low, dims, preferred_element_type=F32)
    return p[:rows] + (p[rows:] + q)


def kernel(
    rhs_hbm, diag_hbm, left_hbm, right_hbm, rank_ref, pattern_ref, row_hbm, col_hbm,
    out_ref,
    rhs, inv, left, right, row, col, sol0, sol1, red, pack, result,
    load_sem, own_sem, unit_send, unit_recv, rhs_send, rhs_recv,
    map_send, map_recv, out_send, out_recv, go_sem,
):
    g = lax.axis_index("blk")
    y = lax.axis_index("rhs")
    places = (g % OCTET, g // OCTET)
    home = (RING // 2) * (g % 2)
    barrier = pltpu.get_barrier_semaphore()

    def unit_copy(unit, origin):
        s, m = ORDER[unit]
        return pltpu.make_async_remote_copy(
            src_ref=diag_hbm.at[s, m],
            dst_ref=inv.at[s, m, pl.ds(SHARE * origin, SHARE), :],
            send_sem=unit_send.at[unit],
            recv_sem=unit_recv.at[unit, (origin - home + RING) % RING - 1],
            device_id=(g, home),
            device_id_type=MESH,
        )

    def rhs_copy(origin):
        return pltpu.make_async_remote_copy(
            src_ref=rhs_hbm,
            dst_ref=rhs.at[pl.ds(ROWS * origin, ROWS), :],
            send_sem=rhs_send,
            recv_sem=rhs_recv.at[(origin - home + RING) % RING - 1],
            device_id=(g, home),
            device_id_type=MESH,
        )

    width = out_ref.shape[1] // PARTS

    def out_copy(part, d):
        n = (home + d) % RING
        return pltpu.make_async_remote_copy(
            src_ref=result.at[pl.ds(ROWS * n, ROWS), pl.ds(part * width, width)],
            dst_ref=out_ref.at[:, pl.ds(part * width, width)],
            send_sem=out_send.at[part, d - 1],
            recv_sem=out_recv.at[part],
            device_id=(g, n),
            device_id_type=MESH,
        )

    @pl.when(y != home)
    def _():
        pl.semaphore_signal(barrier, inc=1, device_id=(g, home), device_id_type=MESH)
        pl.semaphore_wait(barrier, 1)
        rhs_copy(y).start()
        for unit in range(UNITS):
            if unit >= WINDOW and unit % STRIDE == 0:
                pl.semaphore_wait(go_sem, 1)
            unit_copy(unit, y).start()
        rhs_copy(y).wait_send()
        for unit in range(UNITS):
            unit_copy(unit, y).wait_send()
        for part in range(PARTS):
            out_copy(part, 1).wait_recv()

    @pl.when(y == home)
    def _():
        solve_group(
            g, y, places, home, barrier, unit_copy, rhs_copy, out_copy,
            rhs_hbm, diag_hbm, left_hbm, right_hbm, rank_ref, pattern_ref, row_hbm, col_hbm,
            out_ref,
            rhs, inv, left, right, row, col, sol0, sol1, red, pack, result,
            load_sem, own_sem, map_send, map_recv, go_sem,
        )


def solve_group(
    g, y, places, home, barrier, unit_copy, rhs_copy, out_copy,
    rhs_hbm, diag_hbm, left_hbm, right_hbm, rank_ref, pattern_ref, row_hbm, col_hbm,
    out_ref,
    rhs, inv, left, right, row, col, sol0, sol1, red, pack, result,
    load_sem, own_sem, map_send, map_recv, go_sem,
):
    for d in range(1, RING):
        pl.semaphore_signal(
            barrier, inc=1, device_id=(g, (home + d) % RING), device_id_type=MESH
        )

    def peer(stage, d):
        there = (places[stage] + d) % OCTET
        if stage == 0:
            return (places[1] * OCTET + there, (RING // 2) * (there % 2))
        return (there * OCTET + places[0], home)

    for stage in range(2):
        for d in range(1, OCTET):
            pl.semaphore_signal(barrier, inc=1, device_id=peer(stage, d), device_id_type=MESH)

    loads = [[], []]
    loads[0].append(
        pltpu.make_async_copy(rhs_hbm, rhs.at[pl.ds(ROWS * y, ROWS), :], load_sem.at[8])
    )
    for s in range(2):
        for i, (src, dst) in enumerate(
            ((row_hbm, row), (col_hbm, col), (left_hbm, left), (right_hbm, right))
        ):
            loads[s].append(pltpu.make_async_copy(src.at[s], dst.at[s], load_sem.at[4 * s + i]))
        loads[s].append(
            pltpu.make_async_copy(
                diag_hbm.at[s], inv.at[s, :, pl.ds(SHARE * y, SHARE), :], own_sem.at[s]
            )
        )
    for s in range(2):
        for c in loads[s]:
            c.start()

    lane128 = lax.broadcasted_iota(jnp.int32, (8, LANES), 1)
    slot_of, within = lane128 // RANK, lane128 % RANK
    sub128 = lax.broadcasted_iota(jnp.int32, (8, LANES), 0)
    totals = [jnp.zeros((LOWER, LANES), F32), jnp.zeros((UPPER, LANES), F32)]

    def solve(unit):
        s, m = ORDER[unit]
        rows = LOWER if s == 0 else UPPER
        earlier = list(range(m)) if s == 0 else list(range(m + 1, BLOCKS))
        later = list(range(m + 1, BLOCKS)) if s == 0 else list(range(m))
        if s == 0:
            side = jnp.concatenate([rhs[:, m * WIDTH : (m + 1) * WIDTH], -row[0, m]], axis=0)
        else:
            side = jnp.concatenate([sol0[m], -row[1, m]], axis=0)
        if earlier:
            reduced, tiles = [], []
            for h in sorted({(m ^ k) // PACK for k in earlier}):
                ranks = jnp.zeros((8, LANES), jnp.int32)
                piece = jnp.zeros((rows, LANES), F32)
                for j in range(h * PACK, (h + 1) * PACK):
                    k = m ^ j
                    if k not in earlier:
                        tiles.append(jnp.zeros((RANK, WIDTH), F32))
                        continue
                    p = pair_index(m, k)
                    tiles.append(left[s, p])
                    rank = jnp.where(pattern_ref[s, p] == 1, rank_ref[s, p], 0)
                    hit = slot_of == j - h * PACK
                    ranks = jnp.where(hit, rank, ranks)
                    from_k = red[k, :rows, h * LANES : (h + 1) * LANES]
                    piece = jnp.where(jnp.tile(hit, (rows // 8, 1)), from_k, piece)
                keep = jnp.where(within < ranks, 1.0, 0.0).astype(F32)
                reduced.append(piece * jnp.tile(keep, (rows // 8, 1)))
            reduced = jnp.concatenate(reduced, axis=1)
            side = side - times(reduced, jnp.concatenate(tiles, axis=0), False)
        for d in range(1, RING):
            unit_copy(unit, (home + d) % RING).wait_recv()
        if unit == STRIDE - 1:
            pl.semaphore_wait(barrier, RING - 1 + 2 * (OCTET - 1))
        if unit % STRIDE == STRIDE - 1 and unit + WINDOW - STRIDE < UNITS - 1:
            for d in range(1, RING):
                pl.semaphore_signal(
                    go_sem, inc=1, device_id=(g, (home + d) % RING), device_id_type=MESH
                )
        solved = times(side, inv[s, m], True)
        if s == 0:
            sol0[m] = solved
        else:
            sol1[m] = solved
        tiles = [col[s, m]] + [
            right[s, pair_index(m, m ^ j)] if (m ^ j) in later else jnp.zeros((RANK, WIDTH), F32)
            for j in range(1, BLOCKS)
        ]
        count = BLOCKS if any((m ^ k) >= PACK for k in later) else PACK
        onward = times(solved, jnp.concatenate(tiles[:count], axis=0), True)
        if later:
            red[m, :rows, : count * RANK] = onward
        totals[s] = totals[s] + onward[:, :LANES]

    low_lanes = lane128 < RANK
    low_tall = jnp.tile(low_lanes, (ALL // 8, 1))
    unit_pack = jnp.concatenate(
        [
            jnp.where(lane128 % RANK == sub128 + 8 * (lane128 // RANK), 1.0, 0.0).astype(F32),
            jnp.zeros((VROWS, LANES), F32),
        ],
        axis=0,
    )
    only_v = jnp.concatenate([jnp.zeros((8, LANES), F32), jnp.ones((VROWS, LANES), F32)], axis=0)

    def turned(x, groups):
        groups = groups % PACK
        return pltpu.roll(x, RANK * groups, 1) if groups else x

    def beside(x, group_rows):
        x = jnp.where(low_tall[: x.shape[0]], x, 0.0)
        total = x[:group_rows]
        for i in range(1, PACK):
            total = total + turned(x[group_rows * i : group_rows * (i + 1)], i)
        return total

    def packed(gain_rows, v):
        return jnp.concatenate([unit_pack[:8] + beside(gain_rows, 8), beside(v, VROWS)], axis=0)

    def below(v):
        stacked = jnp.concatenate([turned(v, PACK - i) for i in range(PACK)], axis=0)
        return jnp.where(low_tall, stacked, 0.0)

    def spread(m):
        a = m[:8]
        rolled = [turned(a, i) for i in range(PACK)]
        strips = []
        for b in range(PACK):
            for i in range(PACK):
                strips.append(jnp.where(lane128 // RANK == b, rolled[(b - i) % PACK], 0.0))
        return jnp.concatenate(strips, axis=0)

    def after(first, then):
        return times(first, spread(then), False) + then * only_v

    def map_copy(s, stage, d):
        return pltpu.make_async_remote_copy(
            src_ref=pack.at[s, stage, places[stage]],
            dst_ref=pack.at[s, stage, places[stage]],
            send_sem=map_send.at[s, stage, d - 1],
            recv_sem=map_recv.at[s, stage, d - 1],
            device_id=peer(stage, d),
            device_id_type=MESH,
        )

    def map_arrived(s, stage, d):
        here = pack.at[s, stage, (places[stage] + OCTET - d) % OCTET]
        pltpu.make_async_remote_copy(
            src_ref=here,
            dst_ref=here,
            send_sem=map_send.at[s, stage, d - 1],
            recv_sem=map_recv.at[s, stage, d - 1],
            device_id=peer(stage, d),
            device_id_type=MESH,
        ).wait_recv()

    def send_map(s, stage, one):
        pack[s, stage, places[stage]] = one
        for d in range(1, OCTET):
            map_copy(s, stage, d).start()

    def join_maps(s, stage):
        for d in range(1, OCTET):
            map_arrived(s, stage, d)
        mine = places[stage] if s == 0 else OCTET - 1 - places[stage]
        nodes = [pack[s, stage, i if s == 0 else OCTET - 1 - i] for i in range(OCTET)]
        ahead = None
        while len(nodes) > 1:
            left_one = unit_pack
            size = OCTET // len(nodes)
            for i in range(0, len(nodes), 2):
                left_one = jnp.where(mine // size == i + 1, nodes[i], left_one)
            if len(nodes) > 2 or stage == 0:
                nodes = [after(nodes[i], nodes[i + 1]) for i in range(0, len(nodes), 2)]
            else:
                nodes = nodes[:1]
            ahead = left_one if ahead is None else after(left_one, ahead)
        return nodes[0], ahead

    near, carried = None, None
    for unit in range(UNITS):
        if unit == 0:
            for c in loads[0]:
                c.wait()
            for d in range(1, RING):
                rhs_copy((home + d) % RING).wait_recv()
        if unit == BLOCKS:
            for c in loads[1]:
                c.wait()
        solve(unit)
        if unit == BLOCKS - 1:
            send_map(0, 0, packed(totals[0][ALL:], totals[0][:ALL]))
        if unit == BLOCKS + 2:
            whole, near = join_maps(0, 0)
            send_map(0, 1, whole)
        if unit == BLOCKS + 5:
            carried = below(after(join_maps(0, 1)[1], near)[8:])

    early = turned(carried, ALL // RANK)
    upper_v = totals[1][:ALL] + times(early, totals[1], False)
    send_map(1, 0, packed(totals[1][LOWER:], upper_v))
    for m in range(BLOCKS):
        sol1[m, :ALL, :] = sol1[m, :ALL, :] + times(early, sol1[m], False)
    whole, near = join_maps(1, 0)
    send_map(1, 1, whole)
    entering = below(after(join_maps(1, 1)[1], near)[8:])

    late = turned(entering, LOWER // RANK)
    for part in range(PARTS):
        for m in range(part * BLOCKS // PARTS, (part + 1) * BLOCKS // PARTS):
            result[:, m * WIDTH : (m + 1) * WIDTH] = sol1[m, :ALL, :] + times(
                late, sol1[m], False
            )
        for d in range(1, RING):
            out_copy(part, d).start()
    out_ref[...] = result[pl.ds(pl.multiple_of(ROWS * y, ROWS), ROWS), :]

    for s in range(2):
        for stage in range(2):
            for d in range(1, OCTET):
                map_copy(s, stage, d).wait_send()
    for part in range(PARTS):
        for d in range(1, RING):
            out_copy(part, d).wait_send()


def shards(rhs, diag, left, right, rank, pattern, row, col):
    hbm = pl.BlockSpec(memory_space=pl.ANY)
    smem = pl.BlockSpec(memory_space=pltpu.SMEM)
    return pl.pallas_call(
        kernel,
        out_shape=jax.ShapeDtypeStruct(rhs.shape, F32),
        in_specs=[hbm, hbm, hbm, hbm, smem, smem, hbm, hbm],
        out_specs=pl.BlockSpec(memory_space=pltpu.VMEM),
        scratch_shapes=[
            pltpu.VMEM((ALL, rhs.shape[1]), F32),
            pltpu.VMEM((2, BLOCKS, WIDTH, WIDTH), F32),
            pltpu.VMEM(left.shape, F32),
            pltpu.VMEM(right.shape, F32),
            pltpu.VMEM(row.shape, F32),
            pltpu.VMEM(col.shape, F32),
            pltpu.VMEM((BLOCKS, LOWER, WIDTH), F32),
            pltpu.VMEM((BLOCKS, UPPER, WIDTH), F32),
            pltpu.VMEM((BLOCKS, UPPER, WIDTH), F32),
            pltpu.VMEM((2, 2, OCTET, MAP, LANES), F32),
            pltpu.VMEM((ALL, rhs.shape[1]), F32),
            pltpu.SemaphoreType.DMA((9,)),
            pltpu.SemaphoreType.DMA((2,)),
            pltpu.SemaphoreType.DMA((UNITS,)),
            pltpu.SemaphoreType.DMA((UNITS, RING - 1)),
            pltpu.SemaphoreType.DMA,
            pltpu.SemaphoreType.DMA((RING - 1,)),
            pltpu.SemaphoreType.DMA((2, 2, OCTET - 1)),
            pltpu.SemaphoreType.DMA((2, 2, OCTET - 1)),
            pltpu.SemaphoreType.DMA((PARTS, RING - 1)),
            pltpu.SemaphoreType.DMA((PARTS,)),
            pltpu.SemaphoreType.REGULAR,
        ],
        compiler_params=pltpu.CompilerParams(
            collective_id=0, has_side_effects=True, vmem_limit_bytes=60 * 1024 * 1024
        ),
        cost_estimate=pl.CostEstimate(
            flops=400_000_000, bytes_accessed=6_000_000, transcendentals=0
        ),
    )(rhs, diag, left, right, rank, pattern, row, col)


def solution(mesh):
    return jax.shard_map(
        shards,
        mesh=mesh,
        in_specs=(
            P("rhs", "blk"),
            P(None, "blk", "rhs", None),
            P(None, "blk", None, None),
            P(None, "blk", None, None),
            P(None, "blk"),
            P(None, "blk"),
            P(None, "blk", None, None),
            P(None, "blk", None, None),
        ),
        out_specs=P("rhs", "blk"),
        check_vma=False,
    )
```

time: 77.7 us -> 72.9 us (0.938)
  Pallas kernels: 76.1 us -> 71.2 us
    pallas_call x1, Pallas kernels: 76.1 us -> 71.2 us  [shards(): pl.pallas_call(kernel, out_shape=jax.ShapeDtypeStruct(rhs.shape, F32), in...]
where the time goes in v3:
time: 72.9 us; the launch traced here: 72.7 us
  Pallas kernels  71.2 us (98%)
  local copies, waits for them, and re-layouts  1.47 us (2%)
    pallas_call x1, Pallas kernels, shards(): pl.pallas_call(kernel, out_shape=jax.ShapeDtypeStruct(rhs.shape, F32), in...  71.2 us
    unnamed x1, local copies, waits for them, and re-layouts  1.47 us

profile of v3, /device:TPU:1, one launch (start us, length us, event | category | flops | bytes accessed | tf_op | source)
XLA Modules:
  0.0 72.7 jit_solution(6308316510475708406)
XLA Ops:
  0.0 71.2 %shard_map.82 = f32[8,2048]{1,0:T(8,128)} custom-call(f32[8,2048]{1,0:T(8,128)} %rhs_hbm.1, f32[2,8,32,256]{3,2,1,0:T(8,128)} %diag_hbm.1, f32[2,28,32,256]{3,2,1,0:T(8,128)} %left_hbm.1, f32[2,28,32,256]{3,2,1,0:T(8,128)} %right_hbm.1, s32[2,28]{1,0:T(2,128)} %rank_ref.1, s32[2,28]{1,0:T(2,128)} %pattern_ref.1, f32[2,8,32,256]{3,2,1,0:T(8,128)} %row_hbm.1, ...), custom_call_target="tpu_custom_call" | custom-call | flops 400000000 | bytes 6000000 | tf_op jit(solution)/shard_map/pallas_call | solution.py:364
  71.2 1.5 %copy.10 = f32[8,2048]{1,0:T(8,128)} copy(f32[8,2048]{1,0:T(8,128)} %shard_map.82) | data formatting | bytes 131072

commit v4 on v3

--- a/solution.py
+++ b/solution.py
@@ -26,8 +26,12 @@
 PACK = LANES // RANK
 VROWS = ALL // PACK
 MAP = 8 + VROWS
+FAR_FIRST = (4, 5, 3, 6, 2, 7, 1)
 PARTS = 4
-WINDOW = 6
+WINDOW = 8
+RELAYED = (1, 3, 5, 7, 9, 11, 13)
+OPPOSITE, BESIDE = RING // 2, RING // 2 - 1
+DELAY = 2
 STRIDE = 2
 
 ORDER = [(0, m) for m in range(BLOCKS)] + [(1, m) for m in reversed(range(BLOCKS))]
@@ -59,7 +63,7 @@
     out_ref,
     rhs, inv, left, right, row, col, sol0, sol1, red, pack, result,
     load_sem, own_sem, unit_send, unit_recv, rhs_send, rhs_recv,
-    map_send, map_recv, out_send, out_recv, go_sem,
+    map_send, map_recv, out_send, out_recv, go_sem, relay_send, relay_recv,
 ):
     g = lax.axis_index("blk")
     y = lax.axis_index("rhs")
@@ -78,6 +82,20 @@
             device_id_type=MESH,
         )
 
+    far = (home + OPPOSITE) % RING
+
+    def relay_copy(unit, hop):
+        s, m = ORDER[unit]
+        here = inv.at[s, m, pl.ds(SHARE * far, SHARE), :]
+        return pltpu.make_async_remote_copy(
+            src_ref=diag_hbm.at[s, m] if hop == 0 else here,
+            dst_ref=here,
+            send_sem=unit_send.at[unit] if hop == 0 else relay_send.at[unit],
+            recv_sem=relay_recv.at[unit] if hop == 0 else unit_recv.at[unit, OPPOSITE - 1],
+            device_id=(g, (home + BESIDE) % RING if hop == 0 else home),
+            device_id_type=MESH,
+        )
+
     def rhs_copy(origin):
         return pltpu.make_async_remote_copy(
             src_ref=rhs_hbm,
@@ -103,16 +121,46 @@
 
     @pl.when(y != home)
     def _():
+        step = (y - home + RING) % RING
         pl.semaphore_signal(barrier, inc=1, device_id=(g, home), device_id_type=MESH)
-        pl.semaphore_wait(barrier, 1)
+
+        @pl.when(step == BESIDE)
+        def _():
+            pl.semaphore_signal(barrier, inc=1, device_id=(g, far), device_id_type=MESH)
+
+        pl.semaphore_wait(barrier, jnp.where(step == OPPOSITE, 2, 1))
         rhs_copy(y).start()
         for unit in range(UNITS):
             if unit >= WINDOW and unit % STRIDE == 0:
                 pl.semaphore_wait(go_sem, 1)
-            unit_copy(unit, y).start()
+            if unit in RELAYED:
+
+                @pl.when(step == OPPOSITE)
+                def _():
+                    relay_copy(unit, 0).start()
+
+                @pl.when(step != OPPOSITE)
+                def _():
+                    unit_copy(unit, y).start()
+
+            else:
+                unit_copy(unit, y).start()
+            if unit - DELAY in RELAYED:
+
+                @pl.when(step == BESIDE)
+                def _():
+                    relay_copy(unit - DELAY, 0).wait_recv()
+                    relay_copy(unit - DELAY, 1).start()
+
         rhs_copy(y).wait_send()
         for unit in range(UNITS):
             unit_copy(unit, y).wait_send()
+
+        @pl.when(step == BESIDE)
+        def _():
+            for unit in RELAYED:
+                relay_copy(unit, 1).wait_send()
+
         for part in range(PARTS):
             out_copy(part, 1).wait_recv()
 
@@ -345,7 +393,7 @@
             result[:, m * WIDTH : (m + 1) * WIDTH] = sol1[m, :ALL, :] + times(
                 late, sol1[m], False
             )
-        for d in range(1, RING):
+        for d in FAR_FIRST:
             out_copy(part, d).start()
     out_ref[...] = result[pl.ds(pl.multiple_of(ROWS * y, ROWS), ROWS), :]
 
@@ -389,6 +437,8 @@
             pltpu.SemaphoreType.DMA((PARTS, RING - 1)),
             pltpu.SemaphoreType.DMA((PARTS,)),
             pltpu.SemaphoreType.REGULAR,
+            pltpu.SemaphoreType.DMA((UNITS,)),
+            pltpu.SemaphoreType.DMA((UNITS,)),
         ],
         compiler_params=pltpu.CompilerParams(
             collective_id=0, has_side_effects=True, vmem_limit_bytes=60 * 1024 * 1024

time: 72.9 us -> 69.5 us (0.953)
  Pallas kernels: 71.2 us -> 67.8 us
    pallas_call x1, Pallas kernels: 71.2 us -> 67.8 us  [shards(): pl.pallas_call(kernel, out_shape=jax.ShapeDtypeStruct(rhs.shape, F32), in...]
where the time goes in v4:
time: 69.5 us; the launch traced here: 69.3 us
  Pallas kernels  67.8 us (98%)
  local copies, waits for them, and re-layouts  1.47 us (2%)
    pallas_call x1, Pallas kernels, shards(): pl.pallas_call(kernel, out_shape=jax.ShapeDtypeStruct(rhs.shape, F32), in...  67.8 us
    unnamed x1, local copies, waits for them, and re-layouts  1.47 us

profile of v4, /device:TPU:1, one launch (start us, length us, event | category | flops | bytes accessed | tf_op | source)
XLA Modules:
  0.0 69.3 jit_solution(5554002644458984191)
XLA Ops:
  0.0 67.8 %shard_map.82 = f32[8,2048]{1,0:T(8,128)} custom-call(f32[8,2048]{1,0:T(8,128)} %rhs_hbm.1, f32[2,8,32,256]{3,2,1,0:T(8,128)} %diag_hbm.1, f32[2,28,32,256]{3,2,1,0:T(8,128)} %left_hbm.1, f32[2,28,32,256]{3,2,1,0:T(8,128)} %right_hbm.1, s32[2,28]{1,0:T(2,128)} %rank_ref.1, s32[2,28]{1,0:T(2,128)} %pattern_ref.1, f32[2,8,32,256]{3,2,1,0:T(8,128)} %row_hbm.1, ...), custom_call_target="tpu_custom_call" | custom-call | flops 400000000 | bytes 6000000 | tf_op jit(solution)/shard_map/pallas_call | solution.py:412
  67.8 1.5 %copy.10 = f32[8,2048]{1,0:T(8,128)} copy(f32[8,2048]{1,0:T(8,128)} %shard_map.82) | data formatting | bytes 131072

commit v5 on v4

--- a/solution.py
+++ b/solution.py
@@ -27,7 +27,7 @@
 VROWS = ALL // PACK
 MAP = 8 + VROWS
 FAR_FIRST = (4, 5, 3, 6, 2, 7, 1)
-PARTS = 4
+PARTS = 2
 WINDOW = 8
 RELAYED = (1, 3, 5, 7, 9, 11, 13)
 OPPOSITE, BESIDE = RING // 2, RING // 2 - 1

time: 69.5 us -> 69 us (level)
  no operation moved by 1% of the time
where the time goes in v5:
time: 69 us; the launch traced here: 68.7 us
  Pallas kernels  67.2 us (97%)
  local copies, waits for them, and re-layouts  1.47 us (2%)
    pallas_call x1, Pallas kernels, shards(): pl.pallas_call(kernel, out_shape=jax.ShapeDtypeStruct(rhs.shape, F32), in...  67.2 us
    unnamed x1, local copies, waits for them, and re-layouts  1.47 us

profile of v5, /device:TPU:1, one launch (start us, length us, event | category | flops | bytes accessed | tf_op | source)
XLA Modules:
  0.0 68.7 jit_solution(8426533200449864008)
XLA Ops:
  0.0 67.2 %shard_map.82 = f32[8,2048]{1,0:T(8,128)} custom-call(f32[8,2048]{1,0:T(8,128)} %rhs_hbm.1, f32[2,8,32,256]{3,2,1,0:T(8,128)} %diag_hbm.1, f32[2,28,32,256]{3,2,1,0:T(8,128)} %left_hbm.1, f32[2,28,32,256]{3,2,1,0:T(8,128)} %right_hbm.1, s32[2,28]{1,0:T(2,128)} %rank_ref.1, s32[2,28]{1,0:T(2,128)} %pattern_ref.1, f32[2,8,32,256]{3,2,1,0:T(8,128)} %row_hbm.1, ...), custom_call_target="tpu_custom_call" | custom-call | flops 400000000 | bytes 6000000 | tf_op jit(solution)/shard_map/pallas_call | solution.py:412
  67.2 1.5 %copy.10 = f32[8,2048]{1,0:T(8,128)} copy(f32[8,2048]{1,0:T(8,128)} %shard_map.82) | data formatting | bytes 131072

commit v6 on v5

--- a/solution.py
+++ b/solution.py
@@ -250,6 +250,12 @@
                 reduced.append(piece * jnp.tile(keep, (rows // 8, 1)))
             reduced = jnp.concatenate(reduced, axis=1)
             side = side - times(reduced, jnp.concatenate(tiles, axis=0), False)
+        if unit == UNITS - 1:
+            early = turned(carried, ALL // RANK)
+            side = jnp.concatenate([side[:ALL] + times(early, side, False), side[ALL:]], axis=0)
+            totals[s] = jnp.concatenate(
+                [totals[s][:ALL] + times(early, totals[s], False), totals[s][ALL:]], axis=0
+            )
         for d in range(1, RING):
             unit_copy(unit, (home + d) % RING).wait_recv()
         if unit == STRIDE - 1:
@@ -338,7 +344,7 @@
 
     def send_map(s, stage, one):
         pack[s, stage, places[stage]] = one
-        for d in range(1, OCTET):
+        for d in FAR_FIRST:
             map_copy(s, stage, d).start()
 
     def join_maps(s, stage):
@@ -378,14 +384,14 @@
         if unit == BLOCKS + 5:
             carried = below(after(join_maps(0, 1)[1], near)[8:])
 
+    send_map(1, 0, packed(totals[1][LOWER:], totals[1][:ALL]))
     early = turned(carried, ALL // RANK)
-    upper_v = totals[1][:ALL] + times(early, totals[1], False)
-    send_map(1, 0, packed(totals[1][LOWER:], upper_v))
-    for m in range(BLOCKS):
+    for m in range(1, BLOCKS):
         sol1[m, :ALL, :] = sol1[m, :ALL, :] + times(early, sol1[m], False)
     whole, near = join_maps(1, 0)
     send_map(1, 1, whole)
-    entering = below(after(join_maps(1, 1)[1], near)[8:])
+    wide = spread(near)
+    entering = below(times(join_maps(1, 1)[1][8:], wide, False) + near[8:])
 
     late = turned(entering, LOWER // RANK)
     for part in range(PARTS):

time: 69 us -> 69.3 us (level)
  no operation moved by 1% of the time
where the time goes in v6:
time: 69.3 us; the launch traced here: 68.6 us
  Pallas kernels  67.1 us (97%)
  local copies, waits for them, and re-layouts  1.47 us (2%)
    pallas_call x1, Pallas kernels, shards(): pl.pallas_call(kernel, out_shape=jax.ShapeDtypeStruct(rhs.shape, F32), in...  67.1 us
    unnamed x1, local copies, waits for them, and re-layouts  1.47 us

profile of v6, /device:TPU:1, one launch (start us, length us, event | category | flops | bytes accessed | tf_op | source)
XLA Modules:
  0.0 68.6 jit_solution(9843304297360301825)
XLA Ops:
  0.0 67.1 %shard_map.82 = f32[8,2048]{1,0:T(8,128)} custom-call(f32[8,2048]{1,0:T(8,128)} %rhs_hbm.1, f32[2,8,32,256]{3,2,1,0:T(8,128)} %diag_hbm.1, f32[2,28,32,256]{3,2,1,0:T(8,128)} %left_hbm.1, f32[2,28,32,256]{3,2,1,0:T(8,128)} %right_hbm.1, s32[2,28]{1,0:T(2,128)} %rank_ref.1, s32[2,28]{1,0:T(2,128)} %pattern_ref.1, f32[2,8,32,256]{3,2,1,0:T(8,128)} %row_hbm.1, ...), custom_call_target="tpu_custom_call" | custom-call | flops 400000000 | bytes 6000000 | tf_op jit(solution)/shard_map/pallas_call | solution.py:418
  67.1 1.5 %copy.10 = f32[8,2048]{1,0:T(8,128)} copy(f32[8,2048]{1,0:T(8,128)} %shard_map.82) | data formatting | bytes 131072
